TPU v7x, 256 devices: a whole 4x4x8 slice. The times are simulated.
256 devices in a mesh: omega: 8 (over x, core), grid: 32 (over z, y).
Axes of the slice: x: 4, y: 4, z: 8, core: 2. Of those that a mesh axis runs over, the one named last changes fastest.
Arguments:
- vectors: bfloat16 [32, 8, 1024, 1024], P(None, 'omega', 'grid'), may hold values from -6 to 6
- theta_kinetic: bfloat16 [1024, 1024], replicated
- potential: float32 [1024, 1024], P('grid'), may hold values from 0.5 to 3
- phi_coef: float32 [1024], P('grid'), may hold values from 0.3 to 3
- centrifugal: float32 [1024], P('grid'), may hold values from 0.3 to 3
- coriolis: float32 [8, 1024], P('omega', 'grid'), may hold values from 0.5 to 2
- omega_values: int32 [8], P('omega'), may hold values from 0 to 6
Outputs:
- basis: float32 [32, 8, 1024, 1024], P(None, 'omega', 'grid')
- rayleigh: float32 [32, 32], replicated
All inputs are finite; a program needn't handle non-finite values.
Results may differ from a plain program's by a relative error of at most 0.0044.
Values may be sent and summed in bfloat16 or wider, within the bound.
A program may use at most 128 MiB of HBM per device.

v0:
```python
import functools

import jax
import jax.numpy as jnp
import numpy as np
from jax import lax
from jax.experimental import pallas as pl
from jax.experimental.pallas import tpu as pltpu
from jax.sharding import PartitionSpec as P

JTOT = 7
CHUNKS = 4
PH = 32
HALF = 16
F32 = jnp.float32
BF16 = jnp.bfloat16
MESH = pl.DeviceIdType.MESH
HI = lax.Precision.HIGHEST
NN = (((1,), (0,)), ((), ()))
NT = (((1,), (1,)), ((), ()))
TN = (((0,), (0,)), ((), ()))


def phi_table(count):
    row_idx = np.arange(count, dtype=np.int32)[:, None]
    col_idx = np.arange(count, dtype=np.int32)[None, :]
    offset = (row_idx - col_idx) % count
    parity = (1 - 2 * (offset % 2)).astype(np.float32)
    sine = np.sin(np.float32(np.pi) * offset.astype(np.float32) / np.float32(count)).astype(np.float32)
    safe = np.where(offset == 0, np.float32(1.0), sine * sine)
    off_diag = parity / (np.float32(2.0) * safe)
    centre = np.float32((count * count + 2) / 12.0)
    table = np.where(offset == 0, centre, off_diag) * np.float32(12.0 / (count * count))
    return table.astype(jnp.bfloat16)


def dot(a, b, dims=NN):
    return lax.dot_general(a, b, dims, preferred_element_type=F32)


def exact_dot(a, b, dims=NN):
    return lax.dot_general(a, b, dims, precision=HI, preferred_element_type=F32)


def iota(shape, dim):
    return lax.broadcasted_iota(jnp.int32, shape, dim)


def two_parts(x):
    high = x.astype(BF16)
    return high, (x - high.astype(F32)).astype(BF16)


def as_column(row):
    n = row.shape[1]
    wide = jnp.broadcast_to(row, (n, n))
    return jnp.sum(jnp.where(iota((n, n), 0) == iota((n, n), 1), wide, 0.0), axis=1, keepdims=True)


def group_sums(product, inner, outer):
    rows, cols = product.shape
    kept = jnp.where(iota((rows, cols), 0) % inner == iota((rows, cols), 1) % inner, product, 0.0)
    return jnp.sum(kept.reshape(rows // inner, inner, cols), axis=1)


def lane_sums(x, inner, outer):
    lanes = x.shape[1]
    pick = (iota((lanes, outer), 0) // inner == iota((lanes, outer), 1)).astype(F32)
    return exact_dot(x, pick)


def block_diagonal(small, inner, transposed):
    n = small.shape[0]
    full = n * inner
    rows = (iota((full, n), 0) // inner == iota((full, n), 1)).astype(BF16)
    cols = (iota((n, full), 1) // inner == iota((n, full), 0)).astype(BF16)
    tall = dot(rows, small, NT if transposed else NN).astype(BF16)
    wide = dot(tall, cols)
    same = iota((full, full), 0) % inner == iota((full, full), 1) % inner
    return jnp.where(same, wide, 0.0).astype(BF16)


def pack(x):
    return jnp.concatenate([x[8 * a : 8 * a + 8] for a in range(4)], axis=1)


def unpack(x):
    return jnp.concatenate([x[:, 32 * a : 32 * a + 32] for a in range(4)], axis=0)


def main_kernel(
    sizes,
    v_in, t_in, tab_in, pot_in, pc_in, cf_in, co_in, om_in,
    corr_out, gram_out, ray_out,
    vv, tt, tab, pot, pc, cf, co, om,
    perm, send, cols, prod, back, below, above, bond, bond_below, diag, inv, work, racc,
    ar_w, ar_y, ar_z,
    v_sem, in_sem, fs_sem, fr_sem, bs_sem, br_sem, ns_sem, nr_sem, as_sem, ar_sem, out_sem,
):
    nw, ng, ny, nz, cells = sizes
    kk, th, nphi = vv.shape
    kc = kk // CHUNKS
    lanes = kc * PH
    tiles = nphi // 128
    w = lax.axis_index("omega")
    me = lax.axis_index("grid")
    z, y = me // ny, me % ny

    v_copies = [
        pltpu.make_async_copy(v_in.at[pl.ds(c * kc, kc)], vv.at[pl.ds(c * kc, kc)], v_sem.at[c])
        for c in range(CHUNKS)
    ]
    in_copies = [
        pltpu.make_async_copy(src, dst, in_sem.at[i])
        for i, (src, dst) in enumerate(
            ((om_in, om), (co_in, co), (pc_in, pc), (cf_in, cf), (pot_in, pot), (tab_in, tab), (t_in, tt))
        )
    ]
    for copy in v_copies + in_copies:
        copy.start()

    def grid_peer(i):
        return lax.rem(z + i // ny, nz) * ny + lax.rem(y + i % ny, ny)

    barrier = pltpu.get_barrier_semaphore()

    def greet(i, carry):
        pl.semaphore_signal(barrier, inc=1, device_id={"grid": grid_peer(i), "omega": w}, device_id_type=MESH)
        return carry

    lax.fori_loop(1, ng, greet, 0)
    for i in range(1, nw):
        pl.semaphore_signal(
            barrier, inc=1, device_id={"grid": me, "omega": lax.rem(w + i, nw)}, device_id_type=MESH
        )

    source = iota((512, 512), 0)
    target = (source // PH) % 4 * 128 + source // 128 * PH + source % PH
    perm[...] = (target == iota((512, 512), 1)).astype(BF16)

    def to_columns(c):
        spots = [(q, t) for q in range(2) for t in range(tiles)]
        block = vv[pl.ds(c * kc, kc)]
        left = jnp.concatenate(
            [
                jnp.concatenate([block[4 * q + a, :, 128 * t : 128 * t + 128] for a in range(4)], axis=1)
                for q, t in spots
            ],
            axis=0,
        )
        moved = dot(left, perm[...]).astype(BF16)
        for n, (q, t) in enumerate(spots):
            for s in range(4):
                send[c, 4 * t + s, :, 128 * q : 128 * q + 128] = moved[n * th : n * th + th, 128 * s : 128 * s + 128]

    def scatter(c, src, dst, send_sem, recv_sem):
        def one(i, carry):
            peer = grid_peer(i)
            pltpu.make_async_remote_copy(
                src_ref=src.at[c, peer],
                dst_ref=dst.at[c, me],
                send_sem=send_sem.at[c],
                recv_sem=recv_sem.at[c],
                device_id={"grid": peer, "omega": w},
                device_id_type=MESH,
            ).start()
            return carry

        lax.fori_loop(1, ng, one, 0)
        dst[c, me] = src[c, me]

    def wait_all(buf, c, sem):
        rest = buf.at[c, pl.ds(0, ng - 1)]
        pltpu.make_async_copy(rest, rest, sem.at[c]).wait()

    v_copies[0].wait()
    to_columns(0)
    pl.semaphore_wait(barrier, ng - 1 + nw - 1)
    scatter(0, send, cols, fs_sem, fr_sem)
    for c in range(1, CHUNKS):
        v_copies[c].wait()

    def next_chunk(c, carry):
        to_columns(c)
        scatter(c, send, cols, fs_sem, fr_sem)
        return carry

    lax.fori_loop(1, CHUNKS, next_chunk, 0)

    for copy in in_copies:
        copy.wait()
    jtotal = F32(JTOT * (JTOT + 1))
    omega = om[...].astype(F32)
    bond_scale = jnp.sqrt(jtotal - omega * (omega + 1.0)) / JTOT
    cent_factor = (jtotal - 2.0 * omega * omega) / jtotal
    bond[...] = jnp.broadcast_to(as_column(co[...]) * bond_scale, (th, 128))
    up = {"grid": me, "omega": lax.rem(w + 1, nw)}
    down = {"grid": me, "omega": lax.rem(w + nw - 1, nw)}
    sides = [
        pltpu.make_async_remote_copy(
            src_ref=src, dst_ref=dst, send_sem=ns_sem.at[i], recv_sem=nr_sem.at[i], device_id=to, device_id_type=MESH
        )
        for i, (src, dst, to) in enumerate(((vv, below, up), (vv, above, down), (bond, bond_below, up)))
    ]
    for copy in sides:
        copy.start()

    diag[...] = pot[...] + cent_factor * as_column(cf[...])
    inv[...] = 1.0 / (1.0 + pot[...])
    phi_scale = as_column(pc[...])
    wide = min(256, nphi)

    def local_terms(i, carry):
        ks = pl.ds(i // (nphi // wide) * kc, kc)
        ps = pl.ds(pl.multiple_of(i % (nphi // wide) * wide, wide), wide)
        term = dot(vv[ks].reshape(kc * th, nphi), tab[:, ps]).reshape(kc, th, wide)
        work[ks, :, ps] = term * phi_scale[None] + diag[:, ps][None] * vv[ks, :, ps].astype(F32)
        return carry

    lax.fori_loop(0, CHUNKS * (nphi // wide), local_terms, 0)

    def theta_product(c):
        wait_all(cols, c, fr_sem)
        block = cols[c].reshape(ng * th, lanes)
        part = ng // 4

        def rows(i, carry):
            out = dot(tt[pl.ds(i * part * th, part * th)], block).astype(BF16)
            prod[c, pl.ds(i * part, part)] = out.reshape(part, th, lanes)
            return carry

        lax.fori_loop(0, 4, rows, 0)
        scatter(c, prod, back, bs_sem, br_sem)

    def ray_columns(c):
        def pair(i, carry):
            a = jnp.where(i <= c, c, i - c - 1)
            b = jnp.where(i <= c, i, c)
            product = dot(cols[a].reshape(ng * th, lanes), prod[b].reshape(ng * th, lanes), TN)
            racc[b, pl.ds(a * kc, kc)] = group_sums(product, PH, kc)
            return carry

        lax.fori_loop(0, 2 * c + 1, pair, 0)

    theta_product(0)
    ray_columns(0)
    theta_product(1)
    ray_columns(1)

    for copy in sides:
        copy.wait()
    above_factor = jnp.where(w < nw - 1, bond[...], 0.0)[:, :1]
    below_factor = jnp.where(w > 0, bond_below[...], 0.0)[:, :1]

    def couple(i, carry):
        ks = pl.ds(i * 4, 4)
        work[ks] = work[ks] + above_factor[None] * above[ks].astype(F32) + below_factor[None] * below[ks].astype(F32)
        return carry

    lax.fori_loop(0, kk // 4, couple, 0)

    theta_product(2)
    ray_columns(2)

    ray = jnp.zeros((kk, kk), F32)
    for h in range(th // HALF):
        rows = pl.ds(h * HALF, HALF)
        left = vv[:, rows].reshape(kk * HALF, nphi)
        high, low = two_parts(work[:, rows].reshape(kk * HALF, nphi))
        ray = ray + lane_sums(group_sums(dot(left, high, NT) + dot(left, low, NT), HALF, kk), HALF, kk)

    theta_product(3)
    ray_columns(3)

    def all_reduce(a, value):
        stages = (
            (ar_w, nw, w, lambda i: {"grid": me, "omega": i}),
            (ar_y, ny, y, lambda i: {"grid": z * ny + i, "omega": w}),
            (ar_z, nz, z, lambda i: {"grid": i * ny + y, "omega": w}),
        )
        for s, (buf, n, mine, device) in enumerate(stages):
            buf[a, mine] = value
            for i in range(1, n):
                pltpu.make_async_remote_copy(
                    src_ref=buf.at[a, mine],
                    dst_ref=buf.at[a, mine],
                    send_sem=as_sem.at[a, s],
                    recv_sem=ar_sem.at[a, s],
                    device_id=device(lax.rem(mine + i, n)),
                    device_id_type=MESH,
                ).start()
            rest = buf.at[a, pl.ds(0, n - 1)]
            pltpu.make_async_copy(rest, rest, ar_sem.at[a, s]).wait()
            pltpu.make_async_copy(rest, rest, as_sem.at[a, s]).wait()
            value = buf[a, 0]
            for i in range(1, n):
                value = value + buf[a, i]
        return value

    ray_cols = jnp.concatenate([racc[b] for b in range(CHUNKS)], axis=1)
    ray = ray + lane_sums(ray_cols, PH, kk)
    ray = unpack(all_reduce(0, pack(ray))) / cells
    ray_out[...] = ray

    ray_high, ray_low = two_parts(ray)
    mix_high = block_diagonal(ray_high, HALF, True)
    mix_low = block_diagonal(ray_low, HALF, True)

    def project(i, carry):
        rows = pl.ds(pl.multiple_of(i // (nphi // wide) * HALF, HALF), HALF)
        ps = pl.ds(pl.multiple_of(i % (nphi // wide) * wide, wide), wide)
        right = vv[:, rows, ps].reshape(kk * HALF, wide)
        taken = (dot(mix_high, right) + dot(mix_low, right)).reshape(kk, HALF, wide)
        work[:, rows, ps] = work[:, rows, ps] - taken
        return carry

    lax.fori_loop(0, th // HALF * (nphi // wide), project, 0)

    def correct(c, carry):
        wait_all(back, c, br_sem)
        spots = [(q, t) for q in range(2) for t in range(tiles)]
        left = jnp.concatenate(
            [
                jnp.concatenate([back[c, 4 * t + s, :, 128 * q : 128 * q + 128] for s in range(4)], axis=1)
                for q, t in spots
            ],
            axis=0,
        )
        theta = dot(left, perm[...])
        for n, (q, t) in enumerate(spots):
            ps = slice(128 * t, 128 * t + 128)
            for a in range(4):
                k = c * kc + 4 * q + a
                term = theta[n * th : n * th + th, 128 * a : 128 * a + 128]
                work[k, :, ps] = (work[k, :, ps] + term) * inv[:, ps]
        return carry

    lax.fori_loop(0, CHUNKS, correct, 0)

    out_copy = pltpu.make_async_copy(work, corr_out, out_sem)
    out_copy.start()

    gram = jnp.zeros((kk * 8, kk * 8), F32)
    for g in range(th // 8):
        high, low = two_parts(work[:, pl.ds(g * 8, 8)].reshape(kk * 8, nphi))
        gram = gram + dot(high, high, NT) + dot(high, low, NT) + dot(low, high, NT)
    gram = lane_sums(group_sums(gram, 8, kk), 8, kk)
    gram_out[...] = unpack(all_reduce(1, pack(gram))) / cells

    for c in range(CHUNKS):
        wait_all(send, c, fs_sem)
        wait_all(prod, c, bs_sem)
    out_copy.wait()


def basis_kernel(corr_in, gram_in, ray_in, basis_out, ray_out, corr, out, in_sem, out_sem):
    kk, th, nphi = corr.shape
    groups = th // 8
    rows = [pl.ds(8 * g, 8) for g in range(groups)]
    reads = [pltpu.make_async_copy(corr_in.at[:, rows[g]], corr.at[:, rows[g]], in_sem.at[g]) for g in range(groups)]
    writes = [pltpu.make_async_copy(out.at[:, rows[g]], basis_out.at[:, rows[g]], out_sem.at[g]) for g in range(groups)]
    for copy in reads:
        copy.start()
    ray_out[...] = ray_in[...]

    unit = (iota((kk, kk), 0) == iota((kk, kk), 1)).astype(F32)
    table = jnp.concatenate([gram_in[...], unit], axis=1)
    below = iota((kk, 1), 0)
    for j in range(kk - 1):
        pivot = table[j : j + 1]
        factor = jnp.where(below > j, table[:, j : j + 1] / pivot[:, j : j + 1], 0.0)
        table = table - factor * pivot
    scale = jnp.sum(table[:, :kk] * unit, axis=1, keepdims=True)
    factor_inv = table[:, kk:] / jnp.sqrt(scale)

    inv_high, inv_low = two_parts(factor_inv)
    mix_high = block_diagonal(inv_high, 8, False)
    mix_low = block_diagonal(inv_low, 8, False)
    for g in range(groups):
        reads[g].wait()
        high, low = two_parts(corr[:, rows[g]].reshape(kk * 8, nphi))
        res = dot(mix_high, high) + dot(mix_high, low) + dot(mix_low, high)
        out[:, rows[g]] = res.reshape(kk, 8, nphi)
        writes[g].start()
    for copy in writes:
        copy.wait()


def body(vectors, theta_kinetic, potential, phi_coef, centrifugal, coriolis, omega_values):
    kk, _, th, nphi = vectors.shape
    nth = theta_kinetic.shape[0]
    nw, ng = lax.axis_size("omega"), lax.axis_size("grid")
    ny = 4 if ng % 16 == 0 else 2
    nz = ng // ny
    kc = kk // CHUNKS
    cells = nw * nth * nphi
    lanes = kc * PH
    dma = pltpu.SemaphoreType.DMA
    vmem = pltpu.VMEM
    anywhere = pl.BlockSpec(memory_space=pl.ANY)
    local = pl.BlockSpec(memory_space=pltpu.VMEM)
    small = jax.ShapeDtypeStruct((kk, kk), F32)
    blocks = (CHUNKS, ng, th, lanes)
    corr, gram, rayleigh = pl.pallas_call(
        functools.partial(main_kernel, (nw, ng, ny, nz, cells)),
        out_shape=(jax.ShapeDtypeStruct((kk, th, nphi), F32), small, small),
        in_specs=[anywhere] * 8,
        out_specs=(anywhere, local, local),
        scratch_shapes=[
            vmem((kk, th, nphi), BF16), vmem((nth, nth), BF16), vmem((nphi, nphi), BF16), vmem((th, nphi), F32),
            vmem((1, th), F32), vmem((1, th), F32), vmem((1, th), F32), vmem((1, 1), jnp.int32),
            vmem((512, 512), BF16),
            vmem(blocks, BF16), vmem(blocks, BF16), vmem(blocks, BF16), vmem(blocks, BF16),
            vmem((kk, th, nphi), BF16), vmem((kk, th, nphi), BF16),
            vmem((th, 128), F32), vmem((th, 128), F32),
            vmem((th, nphi), F32), vmem((th, nphi), F32),
            vmem((kk, th, nphi), F32),
            vmem((CHUNKS, kk, lanes), F32),
            vmem((2, nw, 8, 128), F32), vmem((2, ny, 8, 128), F32), vmem((2, nz, 8, 128), F32),
            dma((CHUNKS,)), dma((7,)),
            dma((CHUNKS,)), dma((CHUNKS,)), dma((CHUNKS,)), dma((CHUNKS,)),
            dma((3,)), dma((3,)), dma((2, 3)), dma((2, 3)), dma,
        ],
        compiler_params=pltpu.CompilerParams(
            collective_id=0, has_side_effects=True, vmem_limit_bytes=48 * 1024 * 1024
        ),
    )(
        vectors.reshape(kk, th, nphi),
        theta_kinetic,
        jnp.asarray(phi_table(nphi)),
        potential,
        phi_coef.reshape(1, th),
        centrifugal.reshape(1, th),
        coriolis.reshape(1, th),
        omega_values.reshape(1, 1),
    )
    basis, rayleigh = pl.pallas_call(
        basis_kernel,
        out_shape=(jax.ShapeDtypeStruct((kk, th, nphi), F32), small),
        in_specs=[anywhere, local, local],
        out_specs=(anywhere, local),
        scratch_shapes=[vmem((kk, th, nphi), F32), vmem((kk, th, nphi), F32), dma((th // 8,)), dma((th // 8,))],
        compiler_params=pltpu.CompilerParams(vmem_limit_bytes=32 * 1024 * 1024),
    )(corr, gram, rayleigh)
    return basis.reshape(vectors.shape), rayleigh


def solution(mesh):
    placed = (
        P(None, "omega", "grid", None),
        P(),
        P("grid", None),
        P("grid"),
        P("grid"),
        P("omega", "grid"),
        P("omega"),
    )
    return jax.shard_map(
        body,
        mesh=mesh,
        in_specs=placed,
        out_specs=(P(None, "omega", "grid", None), P()),
        check_vma=False,
    )
```

profile of v0, /device:TPU:1, one launch (start us, length us, event | category | flops | bytes accessed | tf_op | source)
XLA Modules:
  0.0 142.5 jit_solution(10663142845068135579)
XLA Ops:
  1.3 0.0 copy-start.1
  1.3 1.6 %copy-done.1 = bf16[32,1,32,1024]{3,2,1,0:T(8,128)(2,1)S(1)} copy-done((bf16[32,1,32,1024]{3,2,1,0:T(8,128)(2,1)S(1)}, bf16[32,1,32,1024]{3,2,1,0:T(8,128)(2,1)}, u32[]{:S(2)}) %copy-start.1) | copy-done | bytes 2097176
  2.9 0.0 copy-start.2
  2.9 1.6 %copy-done.2 = bf16[1024,1024]{1,0:T(8,128)(2,1)S(1)} copy-done((bf16[1024,1024]{1,0:T(8,128)(2,1)S(1)}, bf16[1024,1024]{1,0:T(8,128)(2,1)}, u32[]{:S(2)}) %copy-start.2) | copy-done | bytes 2097176
  4.5 0.0 copy-start.3
  4.5 0.9 copy-done.3
  5.4 0.0 copy-start.4
  5.4 0.7 copy-done.4
  6.0 0.0 copy-start.5
  6.0 0.7 copy-done.5
  6.7 0.0 copy-start.6
  6.7 0.7 copy-done.6
  7.3 125.4 %shard_map.95 = (f32[32,32,1024]{2,1,0:T(8,128)}, f32[32,32]{1,0:T(8,128)S(1)}, f32[32,32]{1,0:T(8,128)S(1)}) custom-call(bf16[32,32,1024]{2,1,0:T(8,128)(2,1)S(1)} %bitcast.8, bf16[1024,1024]{1,0:T(8,128)(2,1)S(1)} %copy-done.2, bf16[1024,1024]{1,0:T(8,128)(2,1)} %constant.2.clone.tab_in, f32[32,1024]{1,0:T(8,128)S(1)} %copy-done.3, f32[1,32]{1,0:T(1,128)S(1)} %bitcast.9, ...), custom_call_target="tpu_custom_call" | custom-call | tf_op jit(solution)/shard_map/pallas_call | solution.py:404
  132.8 0.0 copy-start
  132.8 2.2 %copy-done = f32[32,32,1024]{2,1,0:T(8,128)S(1)} copy-done((f32[32,32,1024]{2,1,0:T(8,128)S(1)}, f32[32,32,1024]{2,1,0:T(8,128)}, u32[]{:S(2)}) %copy-start) | copy-done | bytes 4194328
  134.9 7.6 %shard_map.96 = (f32[32,32,1024]{2,1,0:T(8,128)}, f32[32,32]{1,0:T(8,128)}) custom-call(f32[32,32,1024]{2,1,0:T(8,128)S(1)} %copy-done, f32[32,32]{1,0:T(8,128)S(1)} %get-tuple-element.8.gram_in, f32[32,32]{1,0:T(8,128)S(1)} %get-tuple-element.9.ray_in), custom_call_target="tpu_custom_call" | custom-call | tf_op jit(solution)/shard_map/pallas_call | solution.py:437
Async XLA Ops:
  1.3 1.6 %copy-start.1 = (bf16[32,1,32,1024]{3,2,1,0:T(8,128)(2,1)S(1)}, bf16[32,1,32,1024]{3,2,1,0:T(8,128)(2,1)}, u32[]{:S(2)}) copy-start(bf16[32,1,32,1024]{3,2,1,0:T(8,128)(2,1)} %param.8) | copy-start | bytes 6291460
  2.9 1.6 %copy-start.2 = (bf16[1024,1024]{1,0:T(8,128)(2,1)S(1)}, bf16[1024,1024]{1,0:T(8,128)(2,1)}, u32[]{:S(2)}) copy-start(bf16[1024,1024]{1,0:T(8,128)(2,1)} %t_in.1) | copy-start | bytes 6291460
  4.5 0.9 copy-start.3
  5.4 0.7 copy-start.4
  6.0 0.7 copy-start.5
  6.7 0.7 copy-start.6
  132.8 2.2 %copy-start = (f32[32,32,1024]{2,1,0:T(8,128)S(1)}, f32[32,32,1024]{2,1,0:T(8,128)}, u32[]{:S(2)}) copy-start(f32[32,32,1024]{2,1,0:T(8,128)} %get-tuple-element.7.corr_in) | copy-start | bytes 12582916
where the time goes:
time: 143 us
  Pallas kernels  133 us (93%)
  local copies, waits for them, and re-layouts  8.22 us (6%)
    pallas_call x1, Pallas kernels, body(): pl.pallas_call(functools.partial(main_kernel, (nw, ng, ny, nz, cells)), o...  125 us
    unnamed x14, local copies, waits for them, and re-layouts  8.22 us
    pallas_call x1, Pallas kernels, body(): pl.pallas_call(basis_kernel, out_shape=(jax.ShapeDtypeStruct((kk, th, nph...  7.6 us

commit v1 on v0

--- a/solution.py
+++ b/solution.py
@@ -91,10 +91,10 @@
 def main_kernel(
     sizes,
     v_in, t_in, tab_in, pot_in, pc_in, cf_in, co_in, om_in,
-    corr_out, gram_out, ray_out,
+    high_out, low_out, gram_out, ray_out,
     vv, tt, tab, pot, pc, cf, co, om,
-    perm, send, cols, prod, back, below, above, bond, bond_below, diag, inv, work, racc,
-    ar_w, ar_y, ar_z,
+    perm, send, cols, prod, back, below, above, bond, bond_below, diag, inv, work, racc, high, low,
+    ar_wy, ar_z,
     v_sem, in_sem, fs_sem, fr_sem, bs_sem, br_sem, ns_sem, nr_sem, as_sem, ar_sem, out_sem,
 ):
     nw, ng, ny, nz, cells = sizes
@@ -129,10 +129,12 @@
         return carry
 
     lax.fori_loop(1, ng, greet, 0)
-    for i in range(1, nw):
-        pl.semaphore_signal(
-            barrier, inc=1, device_id={"grid": me, "omega": lax.rem(w + i, nw)}, device_id_type=MESH
-        )
+    def greet_beside(i, carry):
+        peer = {"grid": z * ny + i % ny, "omega": lax.rem(w + i // ny, nw)}
+        pl.semaphore_signal(barrier, inc=1, device_id=peer, device_id_type=MESH)
+        return carry
+
+    lax.fori_loop(ny, nw * ny, greet_beside, 0)
 
     source = iota((512, 512), 0)
     target = (source // PH) % 4 * 128 + source // 128 * PH + source % PH
@@ -175,7 +177,7 @@
 
     v_copies[0].wait()
     to_columns(0)
-    pl.semaphore_wait(barrier, ng - 1 + nw - 1)
+    pl.semaphore_wait(barrier, ng - 1 + (nw - 1) * ny)
     scatter(0, send, cols, fs_sem, fr_sem)
     for c in range(1, CHUNKS):
         v_copies[c].wait()
@@ -230,7 +232,6 @@
             return carry
 
         lax.fori_loop(0, 4, rows, 0)
-        scatter(c, prod, back, bs_sem, br_sem)
 
     def ray_columns(c):
         def pair(i, carry):
@@ -243,6 +244,7 @@
         lax.fori_loop(0, 2 * c + 1, pair, 0)
 
     theta_product(0)
+    scatter(0, prod, back, bs_sem, br_sem)
     ray_columns(0)
     theta_product(1)
     ray_columns(1)
@@ -266,40 +268,49 @@
     for h in range(th // HALF):
         rows = pl.ds(h * HALF, HALF)
         left = vv[:, rows].reshape(kk * HALF, nphi)
-        high, low = two_parts(work[:, rows].reshape(kk * HALF, nphi))
-        ray = ray + lane_sums(group_sums(dot(left, high, NT) + dot(left, low, NT), HALF, kk), HALF, kk)
+        x, x_rest = two_parts(work[:, rows].reshape(kk * HALF, nphi))
+        ray = ray + lane_sums(group_sums(dot(left, x, NT) + dot(left, x_rest, NT), HALF, kk), HALF, kk)
 
     theta_product(3)
     ray_columns(3)
 
-    def all_reduce(a, value):
-        stages = (
-            (ar_w, nw, w, lambda i: {"grid": me, "omega": i}),
-            (ar_y, ny, y, lambda i: {"grid": z * ny + i, "omega": w}),
-            (ar_z, nz, z, lambda i: {"grid": i * ny + y, "omega": w}),
-        )
-        for s, (buf, n, mine, device) in enumerate(stages):
-            buf[a, mine] = value
-            for i in range(1, n):
-                pltpu.make_async_remote_copy(
-                    src_ref=buf.at[a, mine],
-                    dst_ref=buf.at[a, mine],
-                    send_sem=as_sem.at[a, s],
-                    recv_sem=ar_sem.at[a, s],
-                    device_id=device(lax.rem(mine + i, n)),
-                    device_id_type=MESH,
-                ).start()
-            rest = buf.at[a, pl.ds(0, n - 1)]
-            pltpu.make_async_copy(rest, rest, ar_sem.at[a, s]).wait()
-            pltpu.make_async_copy(rest, rest, as_sem.at[a, s]).wait()
-            value = buf[a, 0]
-            for i in range(1, n):
-                value = value + buf[a, i]
-        return value
+    stages = (
+        (ar_wy, nw * ny, w * ny + y, lambda i: {"grid": z * ny + i % ny, "omega": i // ny}),
+        (ar_z, nz, z, lambda i: {"grid": i * ny + y, "omega": w}),
+    )
+
+    def share(a, s, value):
+        buf, n, mine, device = stages[s]
+        buf[a, mine] = value
+
+        def one(i, carry):
+            pltpu.make_async_remote_copy(
+                src_ref=buf.at[a, mine],
+                dst_ref=buf.at[a, mine],
+                send_sem=as_sem.at[a, s],
+                recv_sem=ar_sem.at[a, s],
+                device_id=device(lax.rem(mine + i, n)),
+                device_id_type=MESH,
+            ).start()
+            return carry
+
+        lax.fori_loop(1, n, one, 0)
+
+    def total(a, s):
+        buf, n, _, _ = stages[s]
+        rest = buf.at[a, pl.ds(0, n - 1)]
+        pltpu.make_async_copy(rest, rest, ar_sem.at[a, s]).wait()
+        pltpu.make_async_copy(rest, rest, as_sem.at[a, s]).wait()
+        return jnp.sum(buf[a], axis=0)
 
     ray_cols = jnp.concatenate([racc[b] for b in range(CHUNKS)], axis=1)
     ray = ray + lane_sums(ray_cols, PH, kk)
-    ray = unpack(all_reduce(0, pack(ray))) / cells
+    share(0, 0, pack(ray))
+    scatter(1, prod, back, bs_sem, br_sem)
+    share(0, 1, total(0, 0))
+    scatter(2, prod, back, bs_sem, br_sem)
+    ray = unpack(total(0, 1)) / cells
+    scatter(3, prod, back, bs_sem, br_sem)
     ray_out[...] = ray
 
     ray_high, ray_low = two_parts(ray)
@@ -337,39 +348,59 @@
 
     lax.fori_loop(0, CHUNKS, correct, 0)
 
-    out_copy = pltpu.make_async_copy(work, corr_out, out_sem)
-    out_copy.start()
-
     gram = jnp.zeros((kk * 8, kk * 8), F32)
+    cross = jnp.zeros((kk * 8, kk * 8), F32)
+    out_copies = []
     for g in range(th // 8):
-        high, low = two_parts(work[:, pl.ds(g * 8, 8)].reshape(kk * 8, nphi))
-        gram = gram + dot(high, high, NT) + dot(high, low, NT) + dot(low, high, NT)
+        x, x_rest = two_parts(work[:, pl.ds(g * 8, 8)].reshape(kk * 8, nphi))
+        high[g] = x
+        low[g] = x_rest
+        gram = gram + dot(x, x, NT)
+        cross = cross + dot(x, x_rest, NT)
+        out_copies.append(pltpu.make_async_copy(high.at[g], high_out.at[g], out_sem.at[0, g]))
+        out_copies.append(pltpu.make_async_copy(low.at[g], low_out.at[g], out_sem.at[1, g]))
+        out_copies[-2].start()
+        out_copies[-1].start()
     gram = lane_sums(group_sums(gram, 8, kk), 8, kk)
-    gram_out[...] = unpack(all_reduce(1, pack(gram))) / cells
+    cross = lane_sums(group_sums(cross, 8, kk), 8, kk)
+    unit = (iota((kk, kk), 0) == iota((kk, kk), 1)).astype(F32)
+    gram = gram + cross + exact_dot(unit, cross, NT)
+    share(1, 0, pack(gram))
+    share(1, 1, total(1, 0))
+    gram_out[...] = unpack(total(1, 1)) / cells
 
     for c in range(CHUNKS):
         wait_all(send, c, fs_sem)
         wait_all(prod, c, bs_sem)
-    out_copy.wait()
-
-
-def basis_kernel(corr_in, gram_in, ray_in, basis_out, ray_out, corr, out, in_sem, out_sem):
-    kk, th, nphi = corr.shape
-    groups = th // 8
-    rows = [pl.ds(8 * g, 8) for g in range(groups)]
-    reads = [pltpu.make_async_copy(corr_in.at[:, rows[g]], corr.at[:, rows[g]], in_sem.at[g]) for g in range(groups)]
-    writes = [pltpu.make_async_copy(out.at[:, rows[g]], basis_out.at[:, rows[g]], out_sem.at[g]) for g in range(groups)]
+    for copy in out_copies:
+        copy.wait()
+
+
+def basis_kernel(high_in, low_in, gram_in, ray_in, basis_out, ray_out, high, low, out, in_sem, out_sem):
+    groups, rows, nphi = high.shape
+    kk = rows // 8
+    reads = [
+        pltpu.make_async_copy(src.at[g], dst.at[g], in_sem.at[i, g])
+        for g in range(groups)
+        for i, (src, dst) in enumerate(((high_in, high), (low_in, low)))
+    ]
+    part = [pl.ds(8 * g, 8) for g in range(groups)]
+    writes = [pltpu.make_async_copy(out.at[:, part[g]], basis_out.at[:, part[g]], out_sem.at[g]) for g in range(groups)]
     for copy in reads:
         copy.start()
     ray_out[...] = ray_in[...]
 
     unit = (iota((kk, kk), 0) == iota((kk, kk), 1)).astype(F32)
     table = jnp.concatenate([gram_in[...], unit], axis=1)
-    below = iota((kk, 1), 0)
-    for j in range(kk - 1):
-        pivot = table[j : j + 1]
-        factor = jnp.where(below > j, table[:, j : j + 1] / pivot[:, j : j + 1], 0.0)
-        table = table - factor * pivot
+    row = iota(table.shape, 0)
+    for first in range(0, kk, 4):
+        spread = [jnp.broadcast_to(table[:, j : j + 1], table.shape) for j in range(first, first + 4)]
+        for a in range(4):
+            j = first + a
+            factor = jnp.where(row > j, spread[a] * (1.0 / spread[a][j : j + 1]), 0.0)
+            for b in range(a + 1, 4):
+                spread[b] = spread[b] - factor * spread[b][j : j + 1]
+            table = table - factor * table[j : j + 1]
     scale = jnp.sum(table[:, :kk] * unit, axis=1, keepdims=True)
     factor_inv = table[:, kk:] / jnp.sqrt(scale)
 
@@ -377,10 +408,11 @@
     mix_high = block_diagonal(inv_high, 8, False)
     mix_low = block_diagonal(inv_low, 8, False)
     for g in range(groups):
-        reads[g].wait()
-        high, low = two_parts(corr[:, rows[g]].reshape(kk * 8, nphi))
-        res = dot(mix_high, high) + dot(mix_high, low) + dot(mix_low, high)
-        out[:, rows[g]] = res.reshape(kk, 8, nphi)
+        reads[2 * g].wait()
+        reads[2 * g + 1].wait()
+        x = high[g]
+        res = dot(mix_high, x) + dot(mix_high, low[g]) + dot(mix_low, x)
+        out[:, part[g]] = res.reshape(kk, 8, nphi)
         writes[g].start()
     for copy in writes:
         copy.wait()
@@ -401,11 +433,12 @@
     local = pl.BlockSpec(memory_space=pltpu.VMEM)
     small = jax.ShapeDtypeStruct((kk, kk), F32)
     blocks = (CHUNKS, ng, th, lanes)
-    corr, gram, rayleigh = pl.pallas_call(
+    split = jax.ShapeDtypeStruct((th // 8, kk * 8, nphi), BF16)
+    high, low, gram, rayleigh = pl.pallas_call(
         functools.partial(main_kernel, (nw, ng, ny, nz, cells)),
-        out_shape=(jax.ShapeDtypeStruct((kk, th, nphi), F32), small, small),
+        out_shape=(split, split, small, small),
         in_specs=[anywhere] * 8,
-        out_specs=(anywhere, local, local),
+        out_specs=(anywhere, anywhere, local, local),
         scratch_shapes=[
             vmem((kk, th, nphi), BF16), vmem((nth, nth), BF16), vmem((nphi, nphi), BF16), vmem((th, nphi), F32),
             vmem((1, th), F32), vmem((1, th), F32), vmem((1, th), F32), vmem((1, 1), jnp.int32),
@@ -416,13 +449,14 @@
             vmem((th, nphi), F32), vmem((th, nphi), F32),
             vmem((kk, th, nphi), F32),
             vmem((CHUNKS, kk, lanes), F32),
-            vmem((2, nw, 8, 128), F32), vmem((2, ny, 8, 128), F32), vmem((2, nz, 8, 128), F32),
+            vmem(split.shape, BF16), vmem(split.shape, BF16),
+            vmem((2, nw * ny, 8, 128), F32), vmem((2, nz, 8, 128), F32),
             dma((CHUNKS,)), dma((7,)),
             dma((CHUNKS,)), dma((CHUNKS,)), dma((CHUNKS,)), dma((CHUNKS,)),
-            dma((3,)), dma((3,)), dma((2, 3)), dma((2, 3)), dma,
+            dma((3,)), dma((3,)), dma((2, 2)), dma((2, 2)), dma((2, th // 8)),
         ],
         compiler_params=pltpu.CompilerParams(
-            collective_id=0, has_side_effects=True, vmem_limit_bytes=48 * 1024 * 1024
+            collective_id=0, has_side_effects=True, vmem_limit_bytes=62 * 1024 * 1024
         ),
     )(
         vectors.reshape(kk, th, nphi),
@@ -437,11 +471,14 @@
     basis, rayleigh = pl.pallas_call(
         basis_kernel,
         out_shape=(jax.ShapeDtypeStruct((kk, th, nphi), F32), small),
-        in_specs=[anywhere, local, local],
+        in_specs=[anywhere, anywhere, local, local],
         out_specs=(anywhere, local),
-        scratch_shapes=[vmem((kk, th, nphi), F32), vmem((kk, th, nphi), F32), dma((th // 8,)), dma((th // 8,))],
-        compiler_params=pltpu.CompilerParams(vmem_limit_bytes=32 * 1024 * 1024),
-    )(corr, gram, rayleigh)
+        scratch_shapes=[
+            vmem(split.shape, BF16), vmem(split.shape, BF16), vmem((kk, th, nphi), F32),
+            dma((2, th // 8)), dma((th // 8,)),
+        ],
+        compiler_params=pltpu.CompilerParams(vmem_limit_bytes=62 * 1024 * 1024),
+    )(high, low, gram, rayleigh)
     return basis.reshape(vectors.shape), rayleigh
 
 

time: 143 us -> 128 us (0.90)
  local copies, waits for them, and re-layouts: 8.22 us -> 0 us
  Pallas kernels: 133 us -> 126 us
    unnamed x14 -> x0, local copies, waits for them, and re-layouts: 8.22 us -> none
    pallas_call x1, Pallas kernels: 125 us -> 119 us  [body(): pl.pallas_call(functools.partial(main_kernel, (nw, ng, ny, nz, cells)), o...]
where the time goes in v1:
time: 128 us; the launch traced here: 127 us
  Pallas kernels  126 us (98%)
  between operations  1.29 us (1%)
    pallas_call x1, Pallas kernels, body(): pl.pallas_call(functools.partial(main_kernel, (nw, ng, ny, nz, cells)), o...  119 us
    pallas_call x1, Pallas kernels, body(): pl.pallas_call(basis_kernel, out_shape=(jax.ShapeDtypeStruct((kk, th, nph...  6.59 us

profile of v1, /device:TPU:1, one launch (start us, length us, event | category | flops | bytes accessed | tf_op | source)
XLA Modules:
  0.0 127.3 jit_solution(14210359132985129149)
XLA Ops:
  1.3 119.4 %shard_map.95 = (bf16[4,256,1024]{2,1,0:T(8,128)(2,1)}, bf16[4,256,1024]{2,1,0:T(8,128)(2,1)}, f32[32,32]{1,0:T(8,128)}, f32[32,32]{1,0:T(8,128)}) custom-call(bf16[32,32,1024]{2,1,0:T(8,128)(2,1)} %bitcast.8, bf16[1024,1024]{1,0:T(8,128)(2,1)} %t_in.1, bf16[1024,1024]{1,0:T(8,128)(2,1)} %constant.2.clone.tab_in, f32[32,1024]{1,0:T(8,128)} %pot_in.1, ...), custom_call_target="tpu_custom_call" | custom-call | tf_op jit(solution)/shard_map/pallas_call | solution.py:437
  120.7 6.6 %shard_map.96 = (f32[32,32,1024]{2,1,0:T(8,128)}, f32[32,32]{1,0:T(8,128)}) custom-call(bf16[4,256,1024]{2,1,0:T(8,128)(2,1)} %get-tuple-element.8.high_in, bf16[4,256,1024]{2,1,0:T(8,128)(2,1)} %get-tuple-element.9.low_in, f32[32,32]{1,0:T(8,128)} %get-tuple-element.10.gram_in, f32[32,32]{1,0:T(8,128)} %get-tuple-element.11.ray_in), custom_call_target="tpu_custom_call" | custom-call | tf_op jit(solution)/shard_map/pallas_call | solution.py:471

commit v2 on v1

--- a/solution.py
+++ b/solution.py
@@ -91,11 +91,11 @@
 def main_kernel(
     sizes,
     v_in, t_in, tab_in, pot_in, pc_in, cf_in, co_in, om_in,
-    high_out, low_out, gram_out, ray_out,
+    high, low, gram_out, ray_out,
     vv, tt, tab, pot, pc, cf, co, om,
-    perm, send, cols, prod, back, below, above, bond, bond_below, diag, inv, work, racc, high, low,
+    perm, send, cols, prod, back, below, above, bond, bond_below, diag, inv, work, racc,
     ar_wy, ar_z,
-    v_sem, in_sem, fs_sem, fr_sem, bs_sem, br_sem, ns_sem, nr_sem, as_sem, ar_sem, out_sem,
+    v_sem, in_sem, fs_sem, fr_sem, bs_sem, br_sem, ns_sem, nr_sem, as_sem, ar_sem,
 ):
     nw, ng, ny, nz, cells = sizes
     kk, th, nphi = vv.shape
@@ -116,8 +116,7 @@
             ((om_in, om), (co_in, co), (pc_in, pc), (cf_in, cf), (pot_in, pot), (tab_in, tab), (t_in, tt))
         )
     ]
-    for copy in v_copies + in_copies:
-        copy.start()
+    v_copies[0].start()
 
     def grid_peer(i):
         return lax.rem(z + i // ny, nz) * ny + lax.rem(y + i % ny, ny)
@@ -135,6 +134,9 @@
         return carry
 
     lax.fori_loop(ny, nw * ny, greet_beside, 0)
+
+    for copy in v_copies[1:] + in_copies:
+        copy.start()
 
     source = iota((512, 512), 0)
     target = (source // PH) % 4 * 128 + source // 128 * PH + source % PH
@@ -349,45 +351,28 @@
     lax.fori_loop(0, CHUNKS, correct, 0)
 
     gram = jnp.zeros((kk * 8, kk * 8), F32)
-    cross = jnp.zeros((kk * 8, kk * 8), F32)
-    out_copies = []
     for g in range(th // 8):
         x, x_rest = two_parts(work[:, pl.ds(g * 8, 8)].reshape(kk * 8, nphi))
         high[g] = x
         low[g] = x_rest
-        gram = gram + dot(x, x, NT)
-        cross = cross + dot(x, x_rest, NT)
-        out_copies.append(pltpu.make_async_copy(high.at[g], high_out.at[g], out_sem.at[0, g]))
-        out_copies.append(pltpu.make_async_copy(low.at[g], low_out.at[g], out_sem.at[1, g]))
-        out_copies[-2].start()
-        out_copies[-1].start()
+        both = jnp.concatenate([x, x], axis=1)
+        gram = gram + dot(both, jnp.concatenate([x, x_rest + x_rest], axis=1), NT)
     gram = lane_sums(group_sums(gram, 8, kk), 8, kk)
-    cross = lane_sums(group_sums(cross, 8, kk), 8, kk)
-    unit = (iota((kk, kk), 0) == iota((kk, kk), 1)).astype(F32)
-    gram = gram + cross + exact_dot(unit, cross, NT)
     share(1, 0, pack(gram))
     share(1, 1, total(1, 0))
-    gram_out[...] = unpack(total(1, 1)) / cells
+    gram = unpack(total(1, 1)) / cells
+    gram_out[...] = 0.5 * (gram + gram.T)
 
     for c in range(CHUNKS):
         wait_all(send, c, fs_sem)
         wait_all(prod, c, bs_sem)
-    for copy in out_copies:
-        copy.wait()
-
-
-def basis_kernel(high_in, low_in, gram_in, ray_in, basis_out, ray_out, high, low, out, in_sem, out_sem):
+
+
+def basis_kernel(high, low, gram_in, ray_in, basis_out, ray_out, out, out_sem):
     groups, rows, nphi = high.shape
     kk = rows // 8
-    reads = [
-        pltpu.make_async_copy(src.at[g], dst.at[g], in_sem.at[i, g])
-        for g in range(groups)
-        for i, (src, dst) in enumerate(((high_in, high), (low_in, low)))
-    ]
     part = [pl.ds(8 * g, 8) for g in range(groups)]
     writes = [pltpu.make_async_copy(out.at[:, part[g]], basis_out.at[:, part[g]], out_sem.at[g]) for g in range(groups)]
-    for copy in reads:
-        copy.start()
     ray_out[...] = ray_in[...]
 
     unit = (iota((kk, kk), 0) == iota((kk, kk), 1)).astype(F32)
@@ -408,8 +393,6 @@
     mix_high = block_diagonal(inv_high, 8, False)
     mix_low = block_diagonal(inv_low, 8, False)
     for g in range(groups):
-        reads[2 * g].wait()
-        reads[2 * g + 1].wait()
         x = high[g]
         res = dot(mix_high, x) + dot(mix_high, low[g]) + dot(mix_low, x)
         out[:, part[g]] = res.reshape(kk, 8, nphi)
@@ -433,12 +416,12 @@
     local = pl.BlockSpec(memory_space=pltpu.VMEM)
     small = jax.ShapeDtypeStruct((kk, kk), F32)
     blocks = (CHUNKS, ng, th, lanes)
-    split = jax.ShapeDtypeStruct((th // 8, kk * 8, nphi), BF16)
+    split = vmem((th // 8, kk * 8, nphi), BF16)
     high, low, gram, rayleigh = pl.pallas_call(
         functools.partial(main_kernel, (nw, ng, ny, nz, cells)),
         out_shape=(split, split, small, small),
         in_specs=[anywhere] * 8,
-        out_specs=(anywhere, anywhere, local, local),
+        out_specs=(local, local, local, local),
         scratch_shapes=[
             vmem((kk, th, nphi), BF16), vmem((nth, nth), BF16), vmem((nphi, nphi), BF16), vmem((th, nphi), F32),
             vmem((1, th), F32), vmem((1, th), F32), vmem((1, th), F32), vmem((1, 1), jnp.int32),
@@ -449,35 +432,38 @@
             vmem((th, nphi), F32), vmem((th, nphi), F32),
             vmem((kk, th, nphi), F32),
             vmem((CHUNKS, kk, lanes), F32),
-            vmem(split.shape, BF16), vmem(split.shape, BF16),
             vmem((2, nw * ny, 8, 128), F32), vmem((2, nz, 8, 128), F32),
             dma((CHUNKS,)), dma((7,)),
             dma((CHUNKS,)), dma((CHUNKS,)), dma((CHUNKS,)), dma((CHUNKS,)),
-            dma((3,)), dma((3,)), dma((2, 2)), dma((2, 2)), dma((2, th // 8)),
+            dma((3,)), dma((3,)), dma((2, 2)), dma((2, 2)),
         ],
         compiler_params=pltpu.CompilerParams(
-            collective_id=0, has_side_effects=True, vmem_limit_bytes=62 * 1024 * 1024
+            collective_id=0, has_side_effects=True, vmem_limit_bytes=48 * 1024 * 1024
         ),
     )(
-        vectors.reshape(kk, th, nphi),
-        theta_kinetic,
-        jnp.asarray(phi_table(nphi)),
-        potential,
-        phi_coef.reshape(1, th),
-        centrifugal.reshape(1, th),
-        coriolis.reshape(1, th),
+        *(
+            pltpu.with_memory_space_constraint(x, pltpu.HBM)
+            for x in (
+                vectors.reshape(kk, th, nphi),
+                theta_kinetic,
+                jnp.asarray(phi_table(nphi)),
+                potential,
+                phi_coef.reshape(1, th),
+                centrifugal.reshape(1, th),
+                coriolis.reshape(1, th),
+            )
+        ),
         omega_values.reshape(1, 1),
     )
     basis, rayleigh = pl.pallas_call(
         basis_kernel,
         out_shape=(jax.ShapeDtypeStruct((kk, th, nphi), F32), small),
-        in_specs=[anywhere, anywhere, local, local],
+        in_specs=[local] * 4,
         out_specs=(anywhere, local),
         scratch_shapes=[
-            vmem(split.shape, BF16), vmem(split.shape, BF16), vmem((kk, th, nphi), F32),
-            dma((2, th // 8)), dma((th // 8,)),
+            vmem((kk, th, nphi), F32), dma((th // 8,)),
         ],
-        compiler_params=pltpu.CompilerParams(vmem_limit_bytes=62 * 1024 * 1024),
+        compiler_params=pltpu.CompilerParams(vmem_limit_bytes=32 * 1024 * 1024),
     )(high, low, gram, rayleigh)
     return basis.reshape(vectors.shape), rayleigh
 

time: 128 us -> 125 us (0.977)
  Pallas kernels: 126 us -> 124 us
    pallas_call x1, Pallas kernels: 6.59 us -> 5.09 us  [body(): pl.pallas_call(basis_kernel, out_shape=(jax.ShapeDtypeStruct((kk, th, nph...]
where the time goes in v2:
time: 125 us
  Pallas kernels  124 us (99%)
  between operations  1.29 us (1%)
    pallas_call x1, Pallas kernels, body(): pl.pallas_call(functools.partial(main_kernel, (nw, ng, ny, nz, cells)), o...  118 us
    pallas_call x1, Pallas kernels, body(): pl.pallas_call(basis_kernel, out_shape=(jax.ShapeDtypeStruct((kk, th, nph...  5.09 us

profile of v2, /device:TPU:1, one launch (start us, length us, event | category | flops | bytes accessed | tf_op | source)
XLA Modules:
  0.0 124.8 jit_solution(15306656148275234704)
XLA Ops:
  1.3 118.4 %shard_map.95 = (bf16[4,256,1024]{2,1,0:T(8,128)(2,1)S(1)}, bf16[4,256,1024]{2,1,0:T(8,128)(2,1)S(1)}, f32[32,32]{1,0:T(8,128)S(1)}, f32[32,32]{1,0:T(8,128)S(1)}) custom-call(bf16[32,32,1024]{2,1,0:T(8,128)(2,1)} %bitcast.8, bf16[1024,1024]{1,0:T(8,128)(2,1)} %t_in.1, bf16[1024,1024]{1,0:T(8,128)(2,1)} %constant.2.clone.tab_in, f32[32,1024]{1,0:T(8,128)} %pot_in.1, ...), custom_call_target="tpu_custom_call" | custom-call | tf_op jit(solution)/shard_map/pallas_call | solution.py:420
  119.7 5.1 %shard_map.96 = (f32[32,32,1024]{2,1,0:T(8,128)}, f32[32,32]{1,0:T(8,128)}) custom-call(bf16[4,256,1024]{2,1,0:T(8,128)(2,1)S(1)} %get-tuple-element.8.high, bf16[4,256,1024]{2,1,0:T(8,128)(2,1)S(1)} %get-tuple-element.9.low, f32[32,32]{1,0:T(8,128)S(1)} %get-tuple-element.10.gram_in, f32[32,32]{1,0:T(8,128)S(1)} %get-tuple-element.11.ray_in), custom_call_target="tpu_custom_call" | custom-call | tf_op jit(solution)/shard_map/pallas_call | solution.py:458

commit v3 on v2

--- a/solution.py
+++ b/solution.py
@@ -342,21 +342,25 @@
         theta = dot(left, perm[...])
         for n, (q, t) in enumerate(spots):
             ps = slice(128 * t, 128 * t + 128)
+            done = []
             for a in range(4):
-                k = c * kc + 4 * q + a
                 term = theta[n * th : n * th + th, 128 * a : 128 * a + 128]
-                work[k, :, ps] = (work[k, :, ps] + term) * inv[:, ps]
+                done.append((work[c * kc + 4 * q + a, :, ps] + term) * inv[:, ps])
+            for a in (0, 2):
+                rows = pl.ds(pl.multiple_of((c * kc + 4 * q + a) * 8, 16), 16)
+                for g in range(th // 8):
+                    pair = jnp.concatenate([d[8 * g : 8 * g + 8] for d in done[a : a + 2]], axis=0)
+                    high[g, rows, ps], low[g, rows, ps] = two_parts(pair)
         return carry
 
     lax.fori_loop(0, CHUNKS, correct, 0)
 
     gram = jnp.zeros((kk * 8, kk * 8), F32)
+    cross = jnp.zeros((kk * 8, kk * 8), F32)
     for g in range(th // 8):
-        x, x_rest = two_parts(work[:, pl.ds(g * 8, 8)].reshape(kk * 8, nphi))
-        high[g] = x
-        low[g] = x_rest
-        both = jnp.concatenate([x, x], axis=1)
-        gram = gram + dot(both, jnp.concatenate([x, x_rest + x_rest], axis=1), NT)
+        gram = gram + dot(high[g], high[g], NT)
+        cross = cross + dot(high[g], low[g], NT)
+    gram = gram + cross + cross
     gram = lane_sums(group_sums(gram, 8, kk), 8, kk)
     share(1, 0, pack(gram))
     share(1, 1, total(1, 0))
@@ -371,19 +375,17 @@
 def basis_kernel(high, low, gram_in, ray_in, basis_out, ray_out, out, out_sem):
     groups, rows, nphi = high.shape
     kk = rows // 8
-    part = [pl.ds(8 * g, 8) for g in range(groups)]
-    writes = [pltpu.make_async_copy(out.at[:, part[g]], basis_out.at[:, part[g]], out_sem.at[g]) for g in range(groups)]
     ray_out[...] = ray_in[...]
 
     unit = (iota((kk, kk), 0) == iota((kk, kk), 1)).astype(F32)
     table = jnp.concatenate([gram_in[...], unit], axis=1)
     row = iota(table.shape, 0)
-    for first in range(0, kk, 4):
-        spread = [jnp.broadcast_to(table[:, j : j + 1], table.shape) for j in range(first, first + 4)]
-        for a in range(4):
+    for first in range(0, kk, 16):
+        spread = [jnp.broadcast_to(table[:, j : j + 1], table.shape) for j in range(first, first + 16)]
+        for a in range(16):
             j = first + a
             factor = jnp.where(row > j, spread[a] * (1.0 / spread[a][j : j + 1]), 0.0)
-            for b in range(a + 1, 4):
+            for b in range(a + 1, 16):
                 spread[b] = spread[b] - factor * spread[b][j : j + 1]
             table = table - factor * table[j : j + 1]
     scale = jnp.sum(table[:, :kk] * unit, axis=1, keepdims=True)
@@ -392,11 +394,18 @@
     inv_high, inv_low = two_parts(factor_inv)
     mix_high = block_diagonal(inv_high, 8, False)
     mix_low = block_diagonal(inv_low, 8, False)
+    writes = []
+    wide = nphi // 2
     for g in range(groups):
-        x = high[g]
-        res = dot(mix_high, x) + dot(mix_high, low[g]) + dot(mix_low, x)
-        out[:, part[g]] = res.reshape(kk, 8, nphi)
-        writes[g].start()
+        for t in range(2):
+            ps = slice(t * wide, t * wide + wide)
+            part = slice(8 * g, 8 * g + 8)
+            x = high[g, :, ps]
+            res = dot(mix_high, x) + dot(mix_high, low[g, :, ps]) + dot(mix_low, x)
+            out[:, part, ps] = res.reshape(kk, 8, wide)
+            copy = pltpu.make_async_copy(out.at[:, part, ps], basis_out.at[:, part, ps], out_sem.at[len(writes)])
+            copy.start()
+            writes.append(copy)
     for copy in writes:
         copy.wait()
 
@@ -461,7 +470,7 @@
         in_specs=[local] * 4,
         out_specs=(anywhere, local),
         scratch_shapes=[
-            vmem((kk, th, nphi), F32), dma((th // 8,)),
+            vmem((kk, th, nphi), F32), dma((th // 4,)),
         ],
         compiler_params=pltpu.CompilerParams(vmem_limit_bytes=32 * 1024 * 1024),
     )(high, low, gram, rayleigh)

time: 125 us -> 124 us (level)
  no operation moved by 1% of the time
where the time goes in v3:
time: 124 us
  Pallas kernels  123 us (99%)
  between operations  1.29 us (1%)
    pallas_call x1, Pallas kernels, body(): pl.pallas_call(functools.partial(main_kernel, (nw, ng, ny, nz, cells)), o...  118 us
    pallas_call x1, Pallas kernels, body(): pl.pallas_call(basis_kernel, out_shape=(jax.ShapeDtypeStruct((kk, th, nph...  4.35 us

profile of v3, /device:TPU:1, one launch (start us, length us, event | category | flops | bytes accessed | tf_op | source)
XLA Modules:
  0.0 124.1 jit_solution(471282989655039004)
XLA Ops:
  1.3 118.4 %shard_map.95 = (bf16[4,256,1024]{2,1,0:T(8,128)(2,1)S(1)}, bf16[4,256,1024]{2,1,0:T(8,128)(2,1)S(1)}, f32[32,32]{1,0:T(8,128)S(1)}, f32[32,32]{1,0:T(8,128)S(1)}) custom-call(bf16[32,32,1024]{2,1,0:T(8,128)(2,1)} %bitcast.8, bf16[1024,1024]{1,0:T(8,128)(2,1)} %t_in.1, bf16[1024,1024]{1,0:T(8,128)(2,1)} %constant.2.clone.tab_in, f32[32,1024]{1,0:T(8,128)} %pot_in.1, ...), custom_call_target="tpu_custom_call" | custom-call | tf_op jit(solution)/shard_map/pallas_call | solution.py:429
  119.7 4.3 %shard_map.96 = (f32[32,32,1024]{2,1,0:T(8,128)}, f32[32,32]{1,0:T(8,128)}) custom-call(bf16[4,256,1024]{2,1,0:T(8,128)(2,1)S(1)} %get-tuple-element.8.high, bf16[4,256,1024]{2,1,0:T(8,128)(2,1)S(1)} %get-tuple-element.9.low, f32[32,32]{1,0:T(8,128)S(1)} %get-tuple-element.10.gram_in, f32[32,32]{1,0:T(8,128)S(1)} %get-tuple-element.11.ray_in), custom_call_target="tpu_custom_call" | custom-call | tf_op jit(solution)/shard_map/pallas_call | solution.py:467
